TPU v7x, 32 devices: a whole 2x2x4 slice. The times are simulated.
32 devices in a mesh: row: 16 (over z, x, core), col: 2 (over y).
Axes of the slice: x: 2, y: 2, z: 4, core: 2. Of those that a mesh axis runs over, the one named last changes fastest.
Arguments:
- features: bfloat16 [4096, 128], P(('row', 'col')), may hold values from -6 to 6
- adjacency: bfloat16 [16, 2, 12, 128, 128], P('row', 'col'), may hold values from 0 to 1
- tile_pos: int32 [16, 2, 12], P('row', 'col'), may hold values from 0 to 31, as said below
- tile_count: int32 [16, 2], P('row', 'col'), may hold values from 1 to 12, as said below
- w_self: bfloat16 [128, 256], replicated, may hold values from -0.5 to 0.5
- w_neigh: bfloat16 [128, 256], replicated, may hold values from -0.5 to 0.5
- bias: float32 [256], replicated, may hold values from -3 to 3
- upstream: bfloat16 [4096, 256], P(('row', 'col')), may hold values from -6 to 6
Outputs:
- hidden: bfloat16 [4096, 256], P(('row', 'col'))
- grad_features: bfloat16 [4096, 128], P(('row', 'col'))
- grad_self: float32 [128, 256], replicated
- grad_neigh: float32 [128, 256], replicated
- grad_bias: float32 [256], replicated
Inputs may be any that keep to these rules, and one draw needn't show every extreme that they name: `tile_pos`: the positions of a cell's slots are distinct. Some cell has all 12 slots filled; only the first tile_count slots of a cell count.
All inputs are finite; a program needn't handle non-finite values.
Results may differ from a plain program's by a relative error of at most 0.0075.
Values may be sent and summed in bfloat16 or wider, within the bound.
A program may use at most 64 MiB of HBM per device.

v0:
```python
import math

import jax
import jax.numpy as jnp
from jax import lax
from jax.sharding import PartitionSpec as P


def forward_tiles(adjacency, position, filled, gathered, row_tiles):
    edge_len = adjacency.shape[1]
    col_tiles = gathered.shape[0] // edge_len
    tile_row = position // col_tiles
    tile_col = position % col_tiles
    usable = jnp.arange(position.shape[0]) < filled
    target = jnp.where(usable, tile_row, row_tiles)
    panel_blocks = gathered.reshape(col_tiles, edge_len, gathered.shape[1])[tile_col]
    products = jnp.einsum(
        "tik,tkf->tif", adjacency, panel_blocks, preferred_element_type=jnp.float32
    )
    partial_value = (
        jnp.zeros((row_tiles + 1, edge_len, products.shape[2]), jnp.float32)
        .at[target]
        .add(products)
    )
    partial_value = partial_value[:row_tiles].reshape(row_tiles * edge_len, -1)
    row_weights = jnp.sum(adjacency, axis=2, dtype=jnp.float32)
    degree = jnp.zeros((row_tiles + 1, edge_len), jnp.float32).at[target].add(row_weights)
    return (partial_value, degree[:row_tiles].reshape(-1))


def backward_products(adjacency, position, filled, grad_rows, col_tiles):
    edge_len = adjacency.shape[1]
    row_tiles = grad_rows.shape[0] // edge_len
    tile_row = position // col_tiles
    tile_col = position % col_tiles
    usable = jnp.arange(position.shape[0]) < filled
    target = jnp.where(usable, tile_col, col_tiles)
    row_blocks = grad_rows.reshape(row_tiles, edge_len, grad_rows.shape[1])[tile_row]
    products = jnp.einsum("tik,tif->tkf", adjacency, row_blocks, preferred_element_type=jnp.float32)
    return (products, target)


def weight_sums(features, aggregate, grad_pre, factor):
    local_self = jnp.dot(features.T, grad_pre, preferred_element_type=jnp.float32)
    local_neigh = jnp.dot(aggregate.T, grad_pre, preferred_element_type=jnp.float32)
    local_bias = jnp.sum(grad_pre.astype(jnp.float32), axis=0)
    totals = lax.psum((local_self, local_neigh, local_bias), ("row", "col"))
    return (totals[0] * factor, totals[1] * factor, totals[2] * factor)


def body(features, adjacency, tile_pos, tile_count, w_self, w_neigh, bias, upstream):
    local_adj = adjacency[0, 0]
    position = tile_pos[0, 0]
    filled = tile_count[0, 0]
    edge_len = local_adj.shape[1]
    width = features.shape[1]
    row_count = lax.axis_size("row")
    col_count = lax.axis_size("col")
    row_tiles = features.shape[0] * col_count // edge_len
    col_tiles = features.shape[0] * row_count // edge_len
    gathered = lax.all_gather(features, "row", axis=0, tiled=True)
    partial_value, degree_part = forward_tiles(local_adj, position, filled, gathered, row_tiles)
    summed, degree = (
        lax.psum_scatter(partial_value, "col", scatter_dimension=0, tiled=True),
        lax.psum_scatter(degree_part, "col", scatter_dimension=0, tiled=True),
    )
    inv_root = 1.0 / jnp.sqrt(1.0 + degree)
    aggregate = (summed * inv_root[:, None]).astype(jnp.bfloat16)
    preact = (
        jnp.dot(features, w_self, preferred_element_type=jnp.float32)
        + jnp.dot(aggregate, w_neigh, preferred_element_type=jnp.float32)
        + bias
    )
    gate_s = jax.nn.sigmoid(preact)
    hidden = (preact * gate_s).astype(jnp.bfloat16)
    grad_pre = (upstream.astype(jnp.float32) * (gate_s + preact * gate_s * (1.0 - gate_s))).astype(
        jnp.bfloat16
    )
    factor = 1.0 / math.sqrt(features.shape[0] * row_count * col_count)
    grad_agg = (
        jnp.dot(grad_pre, w_neigh.T, preferred_element_type=jnp.float32) * inv_root[:, None]
    ).astype(jnp.bfloat16)
    grad_rows = lax.all_gather(grad_agg, "col", axis=0, tiled=True)
    products, target = backward_products(local_adj, position, filled, grad_rows, col_tiles)
    back_full = jnp.zeros((col_tiles + 1, edge_len, width), jnp.float32).at[target].add(products)
    back_full = back_full[:col_tiles].reshape(col_tiles * edge_len, width)
    back_terms = lax.psum_scatter(back_full, "row", scatter_dimension=0, tiled=True)
    grad_self, grad_neigh, grad_bias = weight_sums(features, aggregate, grad_pre, factor)
    grad_features = (
        jnp.dot(grad_pre, w_self.T, preferred_element_type=jnp.float32) + back_terms
    ).astype(jnp.bfloat16)
    return (hidden, grad_features, grad_self, grad_neigh, grad_bias)


def solution(mesh):
    placed = (
        P(("row", "col"), None),
        P("row", "col", None, None, None),
        P("row", "col", None),
        P("row", "col"),
        P(),
        P(),
        P(),
        P(("row", "col"), None),
    )
    return jax.shard_map(
        body,
        mesh=mesh,
        in_specs=placed,
        out_specs=(P(("row", "col"), None), P(("row", "col"), None), P(), P(), P()),
        check_vma=False,
    )
```

profile of v0, /device:TPU:0, one launch (start us, length us, event | category | flops | bytes accessed | tf_op | source)
XLA Modules:
  0.0 247.3 jit_solution(18201844037581720807)
XLA Ops:
  7.9 0.7 fusion.12
  8.6 24.8 %all_gather.6 = bf16[2048,128]{1,0:T(8,128)(2,1)S(1)} all-gather(bf16[128,128]{1,0:T(8,128)(2,1)} %param.8), channel_id=1, replica_groups=mesh['row'=16,'col'=2] {'row'}, dimensions={0}, use_global_device_ids=true | all-gather | bytes 557056 | tf_op jit(solution)/shard_map/all_gather | solution.py:61
  33.4 0.6 gather_fusion
  34.0 0.4 convolution_bitcast_fusion.1
  34.5 0.3 copy.26
  34.8 1.4 scatter_fusion
  36.2 0.7 slice.16
  37.0 0.2 convert_reduce_fusion
  37.1 0.6 scatter_custom_fusion.1
  37.8 5.0 %all-reduce = f32[256]{0:T(256)S(1)} all-reduce(f32[256]{0:T(256)S(1)} %slice_bitcast_fusion), channel_id=3, replica_groups=mesh['row'=16,'col'=2] {'col'}, use_global_device_ids=true, to_apply=%region_4.5.clone | all-reduce | flops 256 | bytes 2048
  42.8 0.6 dynamic-slice
  44.1 0.1 fusion.15
  44.2 0.5 reduce-scatter.3.cloned.1.call-done
  44.7 1.8 convert_reduce_fusion.1
  46.5 0.2 fusion.2
  46.7 0.9 convolution_bitcast_fusion.2
  47.5 4.6 %all_gather.7 = bf16[256,128]{1,0:T(8,128)(2,1)S(1)} all-gather(bf16[128,128]{1,0:T(8,128)(2,1)S(1)} %fusion.2), channel_id=1, replica_groups=mesh['row'=16,'col'=2] {'col'}, dimensions={0}, use_global_device_ids=true | all-gather | bytes 98304 | tf_op jit(solution)/shard_map/all_gather | solution.py:83
  52.1 0.6 gather_fusion.1
  52.8 0.9 fusion.14
  53.7 0.3 convolution_bitcast_fusion
  54.1 0.3 copy.28
  54.4 1.4 scatter_fusion.1
  55.8 1.1 slice.17
  56.9 39.3 %psum.23 = f32[256]{0:T(256)S(1)} all-reduce(f32[256]{0:T(256)S(1)} %get-tuple-element.22), channel_id=1, replica_groups=mesh['row'=16,'col'=2] {'row','col'}, use_global_device_ids=true, to_apply=%region_10.11 | all-reduce | flops 256 | bytes 2048 | tf_op jit(solution)/shard_map/psum | solution.py:47
  96.3 0.6 broadcast_multiply_fusion.2
  96.8 82.2 %all-reduce.4.cloned.1.call-done = (f32[128,256]{0,1:T(8,128)}, f32[128,256]{0,1:T(8,128)}) async-done(((f32[128,256]{0,1:T(8,128)}, f32[128,256]{0,1:T(8,128)}), (f32[128,256]{0,1:T(8,128)}, f32[128,256]{0,1:T(8,128)})) %all-reduce.4.cloned.1.call-update) | async-done | bytes 262160 | tf_op jit(solution)/shard_map/psum | solution.py:47
  179.0 0.9 broadcast_multiply_fusion.1
  179.9 0.8 copy.30
  180.7 0.9 broadcast_multiply_fusion
  181.6 0.8 copy.31
  182.4 56.7 %reduce-scatter.5.cloned.1.call-done = f32[128,128]{1,0:T(8,128)} async-done(((f32[2048,128]{1,0:T(8,128)}), f32[128,128]{1,0:T(8,128)}) %reduce-scatter.5.cloned.1.call-update) | async-done | bytes 65552 | tf_op jit(solution)/shard_map/reduce_scatter | solution.py:87
  239.1 1.6 fusion.1
  (29 shorter events, 0.4 us)
Async XLA Ops:
  7.2 37.5 %copy-start = (bf16[128,256]{1,0:T(8,128)(2,1)S(1)}, bf16[128,256]{1,0:T(8,128)(2,1)}, u32[]{:S(2)}) copy-start(bf16[128,256]{1,0:T(8,128)(2,1)} %param.13) | copy-start | bytes 196612
  7.2 26.8 %copy-start.1 = (bf16[1,1,12,128,128]{4,3,2,1,0:T(8,128)(2,1)S(1)}, bf16[1,1,12,128,128]{4,3,2,1,0:T(8,128)(2,1)}, u32[]{:S(2)}) copy-start(bf16[1,1,12,128,128]{4,3,2,1,0:T(8,128)(2,1)} %param.9) | copy-start | bytes 1179652
  7.2 37.5 %reduce-scatter.3.cloned.1.call-start = ((), (), s32[]{:S(2)}) async-start(), calls=%async_computation.2 | async-start | bytes 196608 | tf_op jit(solution)/shard_map/reduce_scatter | solution.py:64
  34.8 8.0 %copy-start.7 = (u32[32]{0:T(128)S(1)}, u32[32]{0:T(128)}, u32[]{:S(2)}) copy-start(u32[32]{0:T(128)} %constant.58) | copy-start | bytes 388
  34.8 9.3 %copy-start.2 = (bf16[128,128]{1,0:T(8,128)(2,1)S(1)}, bf16[128,128]{1,0:T(8,128)(2,1)}, u32[]{:S(2)}) copy-start(bf16[128,128]{1,0:T(8,128)(2,1)} %param.8) | copy-start | bytes 98308
  34.8 9.3 %copy-start.3 = (bf16[128,256]{1,0:T(8,128)(2,1)S(1)}, bf16[128,256]{1,0:T(8,128)(2,1)}, u32[]{:S(2)}) copy-start(bf16[128,256]{1,0:T(8,128)(2,1)} %param.12) | copy-start | bytes 196612
  34.8 9.9 %copy-start.5 = (bf16[128,256]{1,0:T(8,128)(2,1)S(1)}, bf16[128,256]{1,0:T(8,128)(2,1)}, u32[]{:S(2)}) copy-start(bf16[128,256]{1,0:T(8,128)(2,1)} %param.15) | copy-start | bytes 196612
  34.8 9.9 %copy-start.6 = (f32[256]{0:T(256)S(1)}, f32[256]{0:T(256)}, u32[]{:S(2)}) copy-start(f32[256]{0:T(256)} %param.14) | copy-start | bytes 3076
  36.9 142.1 %all-reduce.4.cloned.1.call-start = ((), (), s32[]{:S(2)}) async-start(), calls=%async_computation.4 | async-start | bytes 524288 | tf_op jit(solution)/shard_map/psum | solution.py:47
  44.7 8.0 %copy-start.4 = (f32[128,128]{1,0:T(8,128)S(1)}, f32[128,128]{1,0:T(8,128)}, u32[]{:S(2)}) copy-start(f32[128,128]{1,0:T(8,128)} %reduce-scatter.3.cloned.1.call-done) | copy-start | bytes 196612
  53.7 185.4 %reduce-scatter.5.cloned.1.call-start = ((), (), s32[]{:S(2)}) async-start(), calls=%async_computation.3 | async-start | bytes 1114112 | tf_op jit(solution)/shard_map/reduce_scatter | solution.py:87
Sparse Core Ops, SparseCore 0:
  37.0 7.6 reduce-scatter.2
  53.8 125.1 all-reduce.3
  182.7 56.4 reduce-scatter.4
where the time goes:
time: 248 us; the launch traced here: 247 us
  waiting for transfers between devices  139 us (56%)
  blocking collectives  73.6 us (30%)
  between operations  15.3 us (6%)
  other arithmetic  6.73 us (3%)
  matrix products  6.23 us (3%)
  local copies, waits for them, and re-layouts  5.77 us (2%)
    psum x1, waiting for transfers between devices, weight_sums(): totals = lax.psum((local_self, local_neigh, local_bias), ('row', 'col'))  82.2 us
    reduce_scatter x1, waiting for transfers between devices, body(): lax.psum_scatter(back_full, 'row', scatter_dimension=0, tiled=True)  56.7 us
    psum x1, blocking collectives, weight_sums(): totals = lax.psum((local_self, local_neigh, local_bias), ('row', 'col'))  39.3 us
    all_gather x1, blocking collectives, body(): gathered = lax.all_gather(features, 'row', axis=0, tiled=True)  24.8 us
  transfers between devices with their start and end apart: 3, of which 3 were waited for; matrix products, arithmetic and copies ran while one was open for 4% of the time, Pallas kernels for 0%

commit v1 on v0

v1 whole, which is shorter than its diff:
```python
import functools
import math

import jax
import jax.numpy as jnp
from jax import lax
from jax.experimental import pallas as pl
from jax.experimental.pallas import tpu as pltpu
from jax.sharding import PartitionSpec as P

BF = jnp.bfloat16
F32 = jnp.float32
MESH = pl.DeviceIdType.MESH


def dot(a, b):
    return jnp.dot(a, b, preferred_element_type=F32)


def dot_nt(a, b):
    return lax.dot_general(a, b, (((1,), (1,)), ((), ())), preferred_element_type=F32)


def kernel(
    n_row, n_col, factor,
    feat, adj, pos, cnt, wself, wneigh, bias, up,
    hid_o, gf_o, gs_o, gn_o, gb_o,
    adj_v, dense, gath, f2, up2, w_v, deg, base, inv_row, inv_col, part, agg_v, gpre, pre,
    c_send, c_recv, own, x_send, x_recv, z_send, z_recv,
    g_units, g1_send, g1_recv, g2_send, g2_recv, gfull,
    loc_sem, send_sem, gath_sem, f2_sem, up_sem, deg_sem, part_sem,
    c_sem, x_sem, z_sem, g1_sem, g2_sem, g3_sem, g4_sem,
):
    row = lax.axis_index("row")
    col = lax.axis_index("col")
    depth = n_row // 4
    half = n_row // 2
    core = row % 2
    x = (row // 2) % 2
    z = row // 4
    tile = feat.shape[0]
    slots = adj.shape[2]
    width = feat.shape[1]
    rows = n_col * tile
    units = g_units.shape[0]
    per = units // n_row

    def row_of(dz, dx, dc):
        return (((z + dz) % depth) * 2 + (x + dx) % 2) * 2 + (core + dc) % 2

    def chip(j):
        return row_of(j % depth, j // depth, 0)

    sends = []

    def send(src, dst, sem, to_row, to_col=None):
        copy = pltpu.make_async_remote_copy(
            src_ref=src, dst_ref=dst, send_sem=send_sem.at[len(sends)], recv_sem=sem,
            device_id=(to_row, col if to_col is None else to_col), device_id_type=MESH,
        )
        copy.start()
        sends.append(copy)

    def got(dst, sem):
        pltpu.make_async_remote_copy(
            src_ref=dst, dst_ref=dst, send_sem=send_sem.at[0], recv_sem=sem,
            device_id=(row_of(0, 0, 1), col), device_id_type=MESH,
        ).wait_recv()

    core_peer = row_of(0, 0, 1)
    x_peer = row_of(0, 1, 0)

    barrier = pltpu.get_barrier_semaphore()
    for j in range(1, half):
        pl.semaphore_signal(barrier, inc=1, device_id=(chip(j), col), device_id_type=MESH)
    pl.semaphore_signal(barrier, inc=1, device_id=(core_peer, col), device_id_type=MESH)
    for k in range(1, n_col):
        pl.semaphore_signal(barrier, inc=1, device_id=(row, (col + k) % n_col), device_id_type=MESH)

    own_rows = pl.ds(pl.multiple_of(col * tile, tile), tile)
    locals_ = [
        pltpu.make_async_copy(adj.at[0, 0], adj_v, loc_sem.at[0]),
        pltpu.make_async_copy(feat, gath.at[pl.ds(0, tile)], loc_sem.at[1]),
        pltpu.make_async_copy(feat, f2.at[own_rows], loc_sem.at[2]),
        pltpu.make_async_copy(up, up2.at[own_rows], loc_sem.at[3]),
        pltpu.make_async_copy(wself, w_v.at[0], loc_sem.at[4]),
        pltpu.make_async_copy(wneigh, w_v.at[1], loc_sem.at[5]),
    ]
    for copy in locals_:
        copy.start()
    pl.semaphore_wait(barrier, half - 1 + 1 + n_col - 1)

    def slot(q):
        return gath.at[pl.ds(q * tile, tile)]

    for k in range(1, depth):
        q = depth - k
        send(feat, slot(q), gath_sem.at[q], row_of(k, 0, 0))
    send(feat, slot(depth), gath_sem.at[depth], x_peer)
    send(feat, slot(half), gath_sem.at[half], core_peer)
    for k in range(1, n_col):
        send(feat, f2.at[own_rows], f2_sem.at[n_col - k], row, (col + k) % n_col)
        send(up, up2.at[own_rows], up_sem.at[n_col - k], row, (col + k) % n_col)

    filled = cnt[0, 0]
    places = [jnp.where(t < filled, pos[0, 0, t], -1) for t in range(slots)]
    locals_[0].wait()

    def place(i, carry):
        r = i // n_row
        q = i % n_row
        target = r * n_row + row_of(q % depth, (q % half) // depth, q // half)
        found = jnp.int32(-1)
        for t in range(slots):
            found = jnp.where(places[t] == target, t, found)
        block = adj_v[jnp.maximum(found, 0)]
        keep = jnp.full((tile, tile), found, jnp.int32) >= 0
        block = jnp.where(keep, block.astype(F32), 0.0).astype(BF)
        dense[pl.ds(pl.multiple_of(r * tile, tile), tile), pl.ds(pl.multiple_of(q * tile, tile), tile)] = block
        return carry

    lax.fori_loop(0, n_col * n_row, place, 0)

    for k in range(1, depth):
        q = depth - k
        got(slot(q), gath_sem.at[q])
        send(slot(q), slot(depth + q), gath_sem.at[depth + q], x_peer)
        send(slot(q), slot(half + q), gath_sem.at[half + q], core_peer)

    ones = jnp.ones((16, dense.shape[1]), BF)
    deg[col] = dot_nt(ones, dense[...])[0:8]
    for k in range(1, n_col):
        send(deg.at[col], deg.at[col], deg_sem.at[n_col - k], row, (col + k) % n_col)

    for q in [depth] + [2 * depth - k for k in range(1, depth)]:
        got(slot(q), gath_sem.at[q])
        send(slot(q), slot(half + q), gath_sem.at[half + q], core_peer)

    locals_[1].wait()
    partial_value = dot(dense[:, : half * tile], gath[: half * tile])

    for copy in locals_[2:]:
        copy.wait()
    for k in range(1, n_col):
        sender = (col + k) % n_col
        sender_rows = pl.ds(pl.multiple_of(sender * tile, tile), tile)
        got(f2.at[sender_rows], f2_sem.at[k])
        got(up2.at[sender_rows], up_sem.at[k])
        got(deg.at[sender], deg_sem.at[k])
    base[...] = dot(f2[...], w_v[0]) + bias[...].reshape(1, -1)
    total = deg[0]
    for k in range(1, n_col):
        total = total + deg[k]
    inv_row[...] = 1.0 / jnp.sqrt(1.0 + total)
    for r in range(n_col):
        line = inv_row[0:1, r * tile : (r + 1) * tile]
        inv_col[r * tile : (r + 1) * tile] = jnp.broadcast_to(line, (tile, tile)).T

    for q in range(half, n_row):
        got(slot(q), gath_sem.at[q])
    partial_value += dot(dense[:, half * tile :], gath[half * tile :])
    part[col] = partial_value.astype(BF)
    for k in range(1, n_col):
        send(part.at[col], part.at[col], part_sem.at[n_col - k], row, (col + k) % n_col)
    for k in range(1, n_col):
        got(part.at[(col + k) % n_col], part_sem.at[k])

    summed = part[0].astype(F32)
    for k in range(1, n_col):
        summed = summed + part[k].astype(F32)
    agg_v[...] = (summed * inv_col[...]).astype(BF)
    pre[...] = base[...] + dot(agg_v[...], w_v[1])
    preact = pre[...]
    gate = jax.nn.sigmoid(preact)
    gpre[...] = (up2[...].astype(F32) * (gate + preact * gate * (1.0 - gate))).astype(BF)
    grad_agg = (dot_nt(w_v[1], gpre[...]) * inv_row[0:1]).astype(BF)

    order = list(range(depth, half)) + list(range(depth))
    for j in order[::2]:
        both = dot(grad_agg, dense[:, (half + j) * tile : (half + j + 2) * tile]).astype(BF)
        for i in (0, 1):
            c_send[j + i] = both[:, i * tile : (i + 1) * tile]
            send(c_send.at[j + i], c_recv.at[j + i], c_sem.at[j + i], core_peer)

    gp = gpre[...]
    upper = dot(f2[...].T, gp)
    lower = dot(agg_v[...].T, gp)
    lanes = gp.shape[1] // 128
    for u in range(units):
        r0, l0 = (u // lanes) * 16, (u % lanes) * 128
        src = upper if r0 < width else lower
        g_units[u] = src[r0 % width : r0 % width + 16, l0 : l0 + 128]
    colsum = dot(jnp.ones((8, gp.shape[0]), BF), gp)
    bias_unit = jnp.concatenate([colsum[:, i * 128 : (i + 1) * 128] for i in range(lanes)], axis=0).astype(BF)
    for j in range(half):
        target = row_of(j % depth, j // depth, 1)
        g1_send[j * per : (j + 1) * per] = g_units[pl.ds(target * per, per)].astype(BF)
    g1_send[half * per] = bias_unit
    send(g1_send, g1_recv, g1_sem.at[0], core_peer)

    for j in order[::2]:
        both = dot(grad_agg, dense[:, j * tile : (j + 2) * tile])
        for i in (0, 1):
            own[j + i] = both[:, i * tile : (i + 1) * tile]

    for dz in list(range(1, depth)) + [0]:
        j = depth + dz
        got(c_recv.at[j], c_sem.at[j])
        x_send[dz] = (own[j] + c_recv[j].astype(F32)).astype(BF)
        send(x_send.at[dz], x_recv.at[dz], x_sem.at[dz], x_peer)

    got(g1_recv, g1_sem.at[0])
    for j in list(range(1, half)) + [0]:
        target = chip(j)
        g2_send[j, 0:per] = (
            g_units[pl.ds(target * per, per)] + g1_recv[j * per : (j + 1) * per].astype(F32)
        ).astype(BF)
        g2_send[j, per] = (bias_unit.astype(F32) + g1_recv[half * per].astype(F32)).astype(BF)
        if j:
            back = (j // depth) * depth + (depth - j % depth) % depth
            send(g2_send.at[j], g2_recv.at[back], g2_sem.at[back], target)
        else:
            g2_recv[0] = g2_send[0]

    for dz in list(range(1, depth)) + [0]:
        got(c_recv.at[dz], c_sem.at[dz])
        got(x_recv.at[dz], x_sem.at[dz])
        value = own[dz] + c_recv[dz].astype(F32) + x_recv[dz].astype(F32)
        if dz:
            z_send[dz - 1] = value.astype(BF)
            send(z_send.at[dz - 1], z_recv.at[dz - 1], z_sem.at[dz - 1], row_of(dz, 0, 0))
        else:
            own[0] = value

    for j in range(1, half):
        got(g2_recv.at[j], g2_sem.at[j])
    piece = jnp.zeros(g2_recv.shape[1:], F32)
    for a in range(half):
        rel = ((a % 2 + 2 - x) % 2) * depth + (a // 2 + depth - z) % depth
        piece = piece + g2_recv[rel].astype(F32)
    piece = piece * factor
    gfull[row] = piece[0:per].astype(BF)
    for j in range(1, half):
        back = (j // depth) * depth + (depth - j % depth) % depth
        send(gfull.at[row], gfull.at[row], g3_sem.at[back], chip(j))
    send(gfull.at[row], gfull.at[row], g4_sem.at[0], core_peer)
    sums = piece[per]
    gb_o[...] = jnp.concatenate([sums[i * 8 : i * 8 + 1] for i in range(lanes)], axis=1).reshape(-1)

    preact = pre[own_rows]
    hid_o[...] = (preact * jax.nn.sigmoid(preact)).astype(BF)
    value = own[0]
    for dz in range(1, depth):
        got(z_recv.at[dz - 1], z_sem.at[dz - 1])
        value = value + z_recv[dz - 1].astype(F32)
    gf_o[...] = (dot_nt(gpre[own_rows], w_v[0]) + value.T).astype(BF)

    for j in range(1, half):
        d = chip(j)
        got(gfull.at[d], g3_sem.at[j])
        send(gfull.at[d], gfull.at[d], g4_sem.at[j], core_peer)
    for j in range(half):
        got(gfull.at[row_of(j % depth, j // depth, 1)], g4_sem.at[j])
    for u in range(units):
        r0, l0 = (u // lanes) * 16, (u % lanes) * 128
        out = gs_o if r0 < width else gn_o
        r0 = r0 % width
        out[r0 : r0 + 16, l0 : l0 + 128] = gfull[u // per, u % per].astype(F32)

    for copy in sends:
        copy.wait_send()


def body(features, adjacency, tile_pos, tile_count, w_self, w_neigh, bias, upstream):
    n_row = lax.axis_size("row")
    n_col = lax.axis_size("col")
    tile, width = features.shape
    hidden = upstream.shape[1]
    slots = adjacency.shape[2]
    rows = n_col * tile
    depth, half = n_row // 4, n_row // 2
    units = (2 * width // 16) * (hidden // 128)
    per = units // n_row
    factor = 1.0 / math.sqrt(tile * n_row * n_col)
    sem = pltpu.SemaphoreType.DMA
    n_sends = (
        (depth - 1) + 2 + 2 * (n_col - 1) + 2 * (depth - 1) + (n_col - 1) + depth + (n_col - 1)
        + half + 1 + depth + (half - 1) + (depth - 1) + (half - 1) + half
    )
    any_ = pl.BlockSpec(memory_space=pl.ANY)
    vmem = pl.BlockSpec(memory_space=pltpu.VMEM)
    smem = pl.BlockSpec(memory_space=pltpu.SMEM)
    scratch = [
        pltpu.VMEM((slots, tile, tile), BF),
        pltpu.VMEM((rows, n_row * tile), BF),
        pltpu.VMEM((n_row * tile, width), BF),
        pltpu.VMEM((rows, width), BF),
        pltpu.VMEM((rows, hidden), BF),
        pltpu.VMEM((2, width, hidden), BF),
        pltpu.VMEM((n_col, 8, rows), F32),
        pltpu.VMEM((rows, hidden), F32),
        pltpu.VMEM((8, rows), F32),
        pltpu.VMEM((rows, width), F32),
        pltpu.VMEM((n_col, rows, width), BF),
        pltpu.VMEM((rows, width), BF),
        pltpu.VMEM((rows, hidden), BF),
        pltpu.VMEM((rows, hidden), F32),
        pltpu.VMEM((half, width, tile), BF),
        pltpu.VMEM((half, width, tile), BF),
        pltpu.VMEM((half, width, tile), F32),
        pltpu.VMEM((depth, width, tile), BF),
        pltpu.VMEM((depth, width, tile), BF),
        pltpu.VMEM((depth - 1, width, tile), BF),
        pltpu.VMEM((depth - 1, width, tile), BF),
        pltpu.VMEM((units, 16, 128), F32),
        pltpu.VMEM((half * per + 1, 16, 128), BF),
        pltpu.VMEM((half * per + 1, 16, 128), BF),
        pltpu.VMEM((half, per + 1, 16, 128), BF),
        pltpu.VMEM((half, per + 1, 16, 128), BF),
        pltpu.VMEM((n_row, per, 16, 128), BF),
        sem((6,)), sem((n_sends,)), sem((n_row,)), sem((n_col,)), sem((n_col,)), sem((n_col,)), sem((n_col,)),
        sem((half,)), sem((depth,)), sem((depth,)), sem((1,)), sem((half,)), sem((half,)), sem((half,)),
    ]
    return pl.pallas_call(
        functools.partial(kernel, n_row, n_col, factor),
        out_shape=(
            jax.ShapeDtypeStruct((tile, hidden), BF),
            jax.ShapeDtypeStruct((tile, width), BF),
            jax.ShapeDtypeStruct((width, hidden), F32),
            jax.ShapeDtypeStruct((width, hidden), F32),
            jax.ShapeDtypeStruct((hidden,), F32),
        ),
        in_specs=[any_, any_, smem, smem, any_, any_, vmem, any_],
        out_specs=(vmem,) * 5,
        scratch_shapes=scratch,
        compiler_params=pltpu.CompilerParams(
            collective_id=0, has_side_effects=True, vmem_limit_bytes=48 * 1024 * 1024
        ),
    )(features, adjacency, tile_pos, tile_count, w_self, w_neigh, bias, upstream)


def solution(mesh):
    placed = (
        P(("row", "col"), None),
        P("row", "col", None, None, None),
        P("row", "col", None),
        P("row", "col"),
        P(),
        P(),
        P(),
        P(("row", "col"), None),
    )
    return jax.shard_map(
        body,
        mesh=mesh,
        in_specs=placed,
        out_specs=(P(("row", "col"), None), P(("row", "col"), None), P(), P(), P()),
        check_vma=False,
    )
```

time: 248 us -> 41.9 us (0.17)
  waiting for transfers between devices: 139 us -> 0 us
  blocking collectives: 73.6 us -> 0 us
  Pallas kernels: 0 us -> 32.8 us
  between operations: 15.3 us -> 1.35 us
  other arithmetic: 6.73 us -> 0 us
  matrix products: 6.23 us -> 0 us
    psum x1 -> x0, waiting for transfers between devices: 82.2 us -> none  [weight_sums(): totals = lax.psum((local_self, local_neigh, local_bias), ('row', 'col'))]
    reduce_scatter x2 -> x0, waiting for transfers between devices: 57.2 us -> none  [the longest x1 56.7 us: body(): lax.psum_scatter(back_full, 'row', scatter_dimension=0, tiled=True)]
    psum x1 -> x0, blocking collectives: 39.3 us -> none  [weight_sums(): totals = lax.psum((local_self, local_neigh, local_bias), ('row', 'col'))]
    pallas_call x0 -> x1, Pallas kernels: none -> 32.8 us  [body(): pl.pallas_call(functools.partial(kernel, n_row, n_col, factor), out_shape...]
    all_gather x2 -> x0, blocking collectives: 29.4 us -> none  [the longest x1 24.8 us: body(): gathered = lax.all_gather(features, 'row', axis=0, tiled=True)]
    dot_general x8 -> x0, matrix products: 6.23 us -> none  [the longest x1 1.8 us: body(): jnp.dot(aggregate, w_neigh, preferred_element_type=jnp.float32)]
    unnamed x19, local copies, waits for them, and re-layouts: 2.15 us -> 7.39 us
    unnamed x1 -> x0, blocking collectives: 4.96 us -> none
  transfers between devices with their start and end apart: 3 -> 0, of which waited for: 3 -> 0; matrix products, arithmetic and copies ran while one was open for 4% -> 0% of each run, Pallas kernels for 0% -> 0%
where the time goes in v1:
time: 41.9 us; the launch traced here: 41.5 us
  Pallas kernels  32.8 us (78%)
  local copies, waits for them, and re-layouts  7.39 us (18%)
  between operations  1.35 us (3%)
    pallas_call x1, Pallas kernels, body(): pl.pallas_call(functools.partial(kernel, n_row, n_col, factor), out_shape...  32.8 us
    unnamed x19, local copies, waits for them, and re-layouts  7.39 us

profile of v1, /device:TPU:0, one launch (start us, length us, event | category | flops | bytes accessed | tf_op | source)
XLA Modules:
  0.0 41.5 jit_solution(1127771621548807852)
XLA Ops:
  0.6 0.0 copy-start.5
  0.6 0.0 copy-start.6
  1.3 0.0 copy-done.5
  1.3 0.0 copy-done.6
  1.3 0.0 copy-start
  1.3 1.0 %copy-done = bf16[1,1,12,128,128]{4,3,2,1,0:T(8,128)(2,1)S(1)} copy-done((bf16[1,1,12,128,128]{4,3,2,1,0:T(8,128)(2,1)S(1)}, bf16[1,1,12,128,128]{4,3,2,1,0:T(8,128)(2,1)}, u32[]{:S(2)}) %copy-start) | copy-done | bytes 393240
  2.3 0.0 copy-start.1
  2.3 0.8 %copy-done.1 = bf16[128,256]{1,0:T(8,128)(2,1)S(1)} copy-done((bf16[128,256]{1,0:T(8,128)(2,1)S(1)}, bf16[128,256]{1,0:T(8,128)(2,1)}, u32[]{:S(2)}) %copy-start.1) | copy-done | bytes 65560
  3.2 0.0 copy-start.2
  3.2 0.8 %copy-done.2 = bf16[128,256]{1,0:T(8,128)(2,1)S(1)} copy-done((bf16[128,256]{1,0:T(8,128)(2,1)S(1)}, bf16[128,256]{1,0:T(8,128)(2,1)}, u32[]{:S(2)}) %copy-start.2) | copy-done | bytes 65560
  4.0 0.0 copy-start.3
  4.0 0.8 %copy-done.3 = bf16[128,256]{1,0:T(8,128)(2,1)S(1)} copy-done((bf16[128,256]{1,0:T(8,128)(2,1)S(1)}, bf16[128,256]{1,0:T(8,128)(2,1)}, u32[]{:S(2)}) %copy-start.3) | copy-done | bytes 65560
  4.9 0.0 copy-start.4
  4.9 0.8 %copy-done.4 = bf16[128,128]{1,0:T(8,128)(2,1)S(1)} copy-done((bf16[128,128]{1,0:T(8,128)(2,1)S(1)}, bf16[128,128]{1,0:T(8,128)(2,1)}, u32[]{:S(2)}) %copy-start.4) | copy-done | bytes 32792
  5.6 32.8 %shard_map.119 = (bf16[128,256]{1,0:T(8,128)(2,1)S(1)}, bf16[128,128]{1,0:T(8,128)(2,1)S(1)}, f32[128,256]{1,0:T(8,128)S(1)}, f32[128,256]{1,0:T(8,128)S(1)}, f32[256]{0:T(256)S(1)}) custom-call(bf16[128,128]{1,0:T(8,128)(2,1)S(1)} %copy-done.4, bf16[1,1,12,128,128]{4,3,2,1,0:T(8,128)(2,1)S(1)} %copy-done, s32[1,1,12]{2,1,0:T(1,128)S(1)} %copy-done.6, ...), custom_call_target="tpu_custom_call" | custom-call | tf_op jit(solution)/shard_map/pallas_call | solution.py:324
  38.4 0.6 %copy.19 = bf16[128,256]{1,0:T(8,128)(2,1)} copy(bf16[128,256]{1,0:T(8,128)(2,1)S(1)} %get-tuple-element.10) | data formatting | bytes 131072
  39.0 0.6 %copy.20 = bf16[128,128]{1,0:T(8,128)(2,1)} copy(bf16[128,128]{1,0:T(8,128)(2,1)S(1)} %get-tuple-element.11) | data formatting | bytes 65536
  39.6 0.7 %copy.21 = f32[128,256]{1,0:T(8,128)} copy(f32[128,256]{1,0:T(8,128)S(1)} %get-tuple-element.12) | data formatting | bytes 262144
  40.3 0.7 %copy.22 = f32[128,256]{1,0:T(8,128)} copy(f32[128,256]{1,0:T(8,128)S(1)} %get-tuple-element.13) | data formatting | bytes 262144
  40.9 0.6 %copy.23 = f32[256]{0:T(256)} copy(f32[256]{0:T(256)S(1)} %get-tuple-element.14) | data formatting | bytes 2048
Async XLA Ops:
  0.6 0.7 %copy-start.5 = (f32[256]{0:T(256)S(1)}, f32[256]{0:T(256)}, u32[]{:S(2)}) copy-start(f32[256]{0:T(256)} %bias.1) | copy-start | bytes 3076
  0.6 0.7 %copy-start.6 = (s32[1,1,12]{2,1,0:T(1,128)S(1)}, s32[1,1,12]{2,1,0:T(1,128)}, u32[]{:S(2)}) copy-start(s32[1,1,12]{2,1,0:T(1,128)} %pos.1) | copy-start | bytes 148
  1.3 1.0 %copy-start = (bf16[1,1,12,128,128]{4,3,2,1,0:T(8,128)(2,1)S(1)}, bf16[1,1,12,128,128]{4,3,2,1,0:T(8,128)(2,1)}, u32[]{:S(2)}) copy-start(bf16[1,1,12,128,128]{4,3,2,1,0:T(8,128)(2,1)} %adj.1) | copy-start | bytes 1179652
  2.3 0.8 %copy-start.1 = (bf16[128,256]{1,0:T(8,128)(2,1)S(1)}, bf16[128,256]{1,0:T(8,128)(2,1)}, u32[]{:S(2)}) copy-start(bf16[128,256]{1,0:T(8,128)(2,1)} %wself.1) | copy-start | bytes 196612
  3.2 0.8 %copy-start.2 = (bf16[128,256]{1,0:T(8,128)(2,1)S(1)}, bf16[128,256]{1,0:T(8,128)(2,1)}, u32[]{:S(2)}) copy-start(bf16[128,256]{1,0:T(8,128)(2,1)} %wneigh.1) | copy-start | bytes 196612
  4.0 0.8 %copy-start.3 = (bf16[128,256]{1,0:T(8,128)(2,1)S(1)}, bf16[128,256]{1,0:T(8,128)(2,1)}, u32[]{:S(2)}) copy-start(bf16[128,256]{1,0:T(8,128)(2,1)} %up.1) | copy-start | bytes 196612
  4.9 0.8 %copy-start.4 = (bf16[128,128]{1,0:T(8,128)(2,1)S(1)}, bf16[128,128]{1,0:T(8,128)(2,1)}, u32[]{:S(2)}) copy-start(bf16[128,128]{1,0:T(8,128)(2,1)} %feat.1) | copy-start | bytes 98308

commit v2 on v1

--- a/solution.py
+++ b/solution.py
@@ -23,9 +23,9 @@
 
 def kernel(
     n_row, n_col, factor,
-    feat, adj, pos, cnt, wself, wneigh, bias, up,
+    feat, adj, pos_h, cnt_h, wself, wneigh, bias_h, up,
     hid_o, gf_o, gs_o, gn_o, gb_o,
-    adj_v, dense, gath, f2, up2, w_v, deg, base, inv_row, inv_col, part, agg_v, gpre, pre,
+    pos, cnt, bias, adj_v, dense, gath, f2, up2, w_v, deg, base, inv_row, inv_col, part, agg_v, gpre, pre,
     c_send, c_recv, own, x_send, x_recv, z_send, z_recv,
     g_units, g1_send, g1_recv, g2_send, g2_recv, gfull,
     loc_sem, send_sem, gath_sem, f2_sem, up_sem, deg_sem, part_sem,
@@ -85,6 +85,9 @@
         pltpu.make_async_copy(up, up2.at[own_rows], loc_sem.at[3]),
         pltpu.make_async_copy(wself, w_v.at[0], loc_sem.at[4]),
         pltpu.make_async_copy(wneigh, w_v.at[1], loc_sem.at[5]),
+        pltpu.make_async_copy(bias_h, bias, loc_sem.at[6]),
+        pltpu.make_async_copy(pos_h, pos, loc_sem.at[7]),
+        pltpu.make_async_copy(cnt_h, cnt, loc_sem.at[8]),
     ]
     for copy in locals_:
         copy.start()
@@ -102,6 +105,8 @@
         send(feat, f2.at[own_rows], f2_sem.at[n_col - k], row, (col + k) % n_col)
         send(up, up2.at[own_rows], up_sem.at[n_col - k], row, (col + k) % n_col)
 
+    locals_[7].wait()
+    locals_[8].wait()
     filled = cnt[0, 0]
     places = [jnp.where(t < filled, pos[0, 0, t], -1) for t in range(slots)]
     locals_[0].wait()
@@ -139,7 +144,7 @@
     locals_[1].wait()
     partial_value = dot(dense[:, : half * tile], gath[: half * tile])
 
-    for copy in locals_[2:]:
+    for copy in locals_[2:7]:
         copy.wait()
     for k in range(1, n_col):
         sender = (col + k) % n_col
@@ -269,6 +274,15 @@
 
     for copy in sends:
         copy.wait_send()
+
+
+def write_out(*refs):
+    sems = refs[10]
+    copies = [pltpu.make_async_copy(refs[i], refs[5 + i], sems.at[i]) for i in range(5)]
+    for copy in copies:
+        copy.start()
+    for copy in copies:
+        copy.wait()
 
 
 def body(features, adjacency, tile_pos, tile_count, w_self, w_neigh, bias, upstream):
@@ -287,10 +301,12 @@
         (depth - 1) + 2 + 2 * (n_col - 1) + 2 * (depth - 1) + (n_col - 1) + depth + (n_col - 1)
         + half + 1 + depth + (half - 1) + (depth - 1) + (half - 1) + half
     )
-    any_ = pl.BlockSpec(memory_space=pl.ANY)
+    hbm = pl.BlockSpec(memory_space=pltpu.HBM)
     vmem = pl.BlockSpec(memory_space=pltpu.VMEM)
-    smem = pl.BlockSpec(memory_space=pltpu.SMEM)
     scratch = [
+        pltpu.SMEM(tile_pos.shape, jnp.int32),
+        pltpu.SMEM(tile_count.shape, jnp.int32),
+        pltpu.VMEM(bias.shape, F32),
         pltpu.VMEM((slots, tile, tile), BF),
         pltpu.VMEM((rows, n_row * tile), BF),
         pltpu.VMEM((n_row * tile, width), BF),
@@ -318,25 +334,33 @@
         pltpu.VMEM((half, per + 1, 16, 128), BF),
         pltpu.VMEM((half, per + 1, 16, 128), BF),
         pltpu.VMEM((n_row, per, 16, 128), BF),
-        sem((6,)), sem((n_sends,)), sem((n_row,)), sem((n_col,)), sem((n_col,)), sem((n_col,)), sem((n_col,)),
+        sem((9,)), sem((n_sends,)), sem((n_row,)), sem((n_col,)), sem((n_col,)), sem((n_col,)), sem((n_col,)),
         sem((half,)), sem((depth,)), sem((depth,)), sem((1,)), sem((half,)), sem((half,)), sem((half,)),
     ]
-    return pl.pallas_call(
+    shapes = (
+        jax.ShapeDtypeStruct((tile, hidden), BF),
+        jax.ShapeDtypeStruct((tile, width), BF),
+        jax.ShapeDtypeStruct((width, hidden), F32),
+        jax.ShapeDtypeStruct((width, hidden), F32),
+        jax.ShapeDtypeStruct((hidden,), F32),
+    )
+    results = pl.pallas_call(
         functools.partial(kernel, n_row, n_col, factor),
-        out_shape=(
-            jax.ShapeDtypeStruct((tile, hidden), BF),
-            jax.ShapeDtypeStruct((tile, width), BF),
-            jax.ShapeDtypeStruct((width, hidden), F32),
-            jax.ShapeDtypeStruct((width, hidden), F32),
-            jax.ShapeDtypeStruct((hidden,), F32),
-        ),
-        in_specs=[any_, any_, smem, smem, any_, any_, vmem, any_],
+        out_shape=shapes,
+        in_specs=[hbm] * 8,
         out_specs=(vmem,) * 5,
         scratch_shapes=scratch,
         compiler_params=pltpu.CompilerParams(
-            collective_id=0, has_side_effects=True, vmem_limit_bytes=48 * 1024 * 1024
+            collective_id=0, has_side_effects=True, vmem_limit_bytes=62 * 1024 * 1024
         ),
     )(features, adjacency, tile_pos, tile_count, w_self, w_neigh, bias, upstream)
+    return pl.pallas_call(
+        write_out,
+        out_shape=shapes,
+        in_specs=[vmem] * 5,
+        out_specs=(hbm,) * 5,
+        scratch_shapes=[sem((5,))],
+    )(*results)
 
 
 def solution(mesh):

time: 41.9 us -> 36.5 us (0.87)
  local copies, waits for them, and re-layouts: 7.39 us -> 0 us
  Pallas kernels: 32.8 us -> 35 us
    unnamed x19 -> x0, local copies, waits for them, and re-layouts: 7.39 us -> none
    pallas_call x0 -> x1, Pallas kernels: none -> 1.8 us  [body(): pl.pallas_call(write_out, out_shape=shapes, in_specs=[vmem] * 5, out_spec...]
    pallas_call x1, Pallas kernels: 32.8 us -> 33.2 us  [body(): pl.pallas_call(functools.partial(kernel, n_row, n_col, factor), out_shape...]
where the time goes in v2:
time: 36.5 us; the launch traced here: 36.3 us
  Pallas kernels  35 us (96%)
  between operations  1.29 us (4%)
    pallas_call x1, Pallas kernels, body(): pl.pallas_call(functools.partial(kernel, n_row, n_col, factor), out_shape...  33.2 us
    pallas_call x1, Pallas kernels, body(): pl.pallas_call(write_out, out_shape=shapes, in_specs=[vmem] * 5, out_spec...  1.8 us

profile of v2, /device:TPU:0, one launch (start us, length us, event | category | flops | bytes accessed | tf_op | source)
XLA Modules:
  0.0 36.3 jit_solution(17280098887780836698)
XLA Ops:
  1.3 33.2 %shard_map.119 = (bf16[128,256]{1,0:T(8,128)(2,1)}, bf16[128,128]{1,0:T(8,128)(2,1)}, f32[128,256]{1,0:T(8,128)}, f32[128,256]{1,0:T(8,128)}, f32[256]{0:T(256)}) custom-call(bf16[128,128]{1,0:T(8,128)(2,1)} %feat.1, bf16[1,1,12,128,128]{4,3,2,1,0:T(8,128)(2,1)} %adj.1, s32[1,1,12]{2,1,0:T(1,128)} %pos_h.1, s32[1,1]{1,0:T(1,128)S(6)} %copy.13.cnt_h, ...), custom_call_target="tpu_custom_call" | custom-call | tf_op jit(solution)/shard_map/pallas_call | solution.py:347
  34.5 1.8 %shard_map.120 = (bf16[128,256]{1,0:T(8,128)(2,1)}, bf16[128,128]{1,0:T(8,128)(2,1)}, f32[128,256]{1,0:T(8,128)}, f32[128,256]{1,0:T(8,128)}, f32[256]{0:T(256)}) custom-call(bf16[128,256]{1,0:T(8,128)(2,1)} %get-tuple-element.10.refs_0_, bf16[128,128]{1,0:T(8,128)(2,1)} %get-tuple-element.11.refs_1_, f32[128,256]{1,0:T(8,128)} %get-tuple-element.12.refs_2_, ...), custom_call_target="tpu_custom_call" | custom-call | tf_op jit(solution)/shard_map/pallas_call | solution.py:357

commit v3 on v2

--- a/solution.py
+++ b/solution.py
@@ -107,7 +107,7 @@
 
     locals_[7].wait()
     locals_[8].wait()
-    filled = cnt[0, 0]
+    filled = cnt[0, 0, 0]
     places = [jnp.where(t < filled, pos[0, 0, t], -1) for t in range(slots)]
     locals_[0].wait()
 
@@ -132,8 +132,7 @@
         send(slot(q), slot(depth + q), gath_sem.at[depth + q], x_peer)
         send(slot(q), slot(half + q), gath_sem.at[half + q], core_peer)
 
-    ones = jnp.ones((16, dense.shape[1]), BF)
-    deg[col] = dot_nt(ones, dense[...])[0:8]
+    deg[col] = dot(dense[...], jnp.ones((dense.shape[1], tile), BF)).T[0:8]
     for k in range(1, n_col):
         send(deg.at[col], deg.at[col], deg_sem.at[n_col - k], row, (col + k) % n_col)
 
@@ -144,6 +143,12 @@
     locals_[1].wait()
     partial_value = dot(dense[:, : half * tile], gath[: half * tile])
 
+    for q in range(half, n_row):
+        got(slot(q), gath_sem.at[q])
+    partial_value += dot(dense[:, half * tile :], gath[half * tile :])
+    part[col] = partial_value.astype(BF)
+    for k in range(1, n_col):
+        send(part.at[col], part.at[col], part_sem.at[n_col - k], row, (col + k) % n_col)
     for copy in locals_[2:7]:
         copy.wait()
     for k in range(1, n_col):
@@ -161,12 +166,6 @@
         line = inv_row[0:1, r * tile : (r + 1) * tile]
         inv_col[r * tile : (r + 1) * tile] = jnp.broadcast_to(line, (tile, tile)).T
 
-    for q in range(half, n_row):
-        got(slot(q), gath_sem.at[q])
-    partial_value += dot(dense[:, half * tile :], gath[half * tile :])
-    part[col] = partial_value.astype(BF)
-    for k in range(1, n_col):
-        send(part.at[col], part.at[col], part_sem.at[n_col - k], row, (col + k) % n_col)
     for k in range(1, n_col):
         got(part.at[(col + k) % n_col], part_sem.at[k])
 
@@ -179,13 +178,6 @@
     gate = jax.nn.sigmoid(preact)
     gpre[...] = (up2[...].astype(F32) * (gate + preact * gate * (1.0 - gate))).astype(BF)
     grad_agg = (dot_nt(w_v[1], gpre[...]) * inv_row[0:1]).astype(BF)
-
-    order = list(range(depth, half)) + list(range(depth))
-    for j in order[::2]:
-        both = dot(grad_agg, dense[:, (half + j) * tile : (half + j + 2) * tile]).astype(BF)
-        for i in (0, 1):
-            c_send[j + i] = both[:, i * tile : (i + 1) * tile]
-            send(c_send.at[j + i], c_recv.at[j + i], c_sem.at[j + i], core_peer)
 
     gp = gpre[...]
     upper = dot(f2[...].T, gp)
@@ -203,16 +195,17 @@
     g1_send[half * per] = bias_unit
     send(g1_send, g1_recv, g1_sem.at[0], core_peer)
 
+    order = list(range(depth, half)) + list(range(depth))
+    for j in order[::2]:
+        both = dot(grad_agg, dense[:, (half + j) * tile : (half + j + 2) * tile]).astype(BF)
+        for i in (0, 1):
+            c_send[j + i] = both[:, i * tile : (i + 1) * tile]
+            send(c_send.at[j + i], c_recv.at[j + i], c_sem.at[j + i], core_peer)
+
     for j in order[::2]:
         both = dot(grad_agg, dense[:, j * tile : (j + 2) * tile])
         for i in (0, 1):
             own[j + i] = both[:, i * tile : (i + 1) * tile]
-
-    for dz in list(range(1, depth)) + [0]:
-        j = depth + dz
-        got(c_recv.at[j], c_sem.at[j])
-        x_send[dz] = (own[j] + c_recv[j].astype(F32)).astype(BF)
-        send(x_send.at[dz], x_recv.at[dz], x_sem.at[dz], x_peer)
 
     got(g1_recv, g1_sem.at[0])
     for j in list(range(1, half)) + [0]:
@@ -226,6 +219,12 @@
             send(g2_send.at[j], g2_recv.at[back], g2_sem.at[back], target)
         else:
             g2_recv[0] = g2_send[0]
+
+    for dz in list(range(1, depth)) + [0]:
+        j = depth + dz
+        got(c_recv.at[j], c_sem.at[j])
+        x_send[dz] = (own[j] + c_recv[j].astype(F32)).astype(BF)
+        send(x_send.at[dz], x_recv.at[dz], x_sem.at[dz], x_peer)
 
     for dz in list(range(1, depth)) + [0]:
         got(c_recv.at[dz], c_sem.at[dz])
@@ -305,7 +304,7 @@
     vmem = pl.BlockSpec(memory_space=pltpu.VMEM)
     scratch = [
         pltpu.SMEM(tile_pos.shape, jnp.int32),
-        pltpu.SMEM(tile_count.shape, jnp.int32),
+        pltpu.SMEM((1, 1, 1), jnp.int32),
         pltpu.VMEM(bias.shape, F32),
         pltpu.VMEM((slots, tile, tile), BF),
         pltpu.VMEM((rows, n_row * tile), BF),
@@ -353,7 +352,7 @@
         compiler_params=pltpu.CompilerParams(
             collective_id=0, has_side_effects=True, vmem_limit_bytes=62 * 1024 * 1024
         ),
-    )(features, adjacency, tile_pos, tile_count, w_self, w_neigh, bias, upstream)
+    )(features, adjacency, tile_pos, tile_count.reshape(1, 1, 1), w_self, w_neigh, bias, upstream)
     return pl.pallas_call(
         write_out,
         out_shape=shapes,

time: 36.5 us -> 36.2 us (level)
  no operation moved by 1% of the time
where the time goes in v3:
time: 36.2 us; the launch traced here: 36 us
  Pallas kernels  34.7 us (96%)
  between operations  1.29 us (4%)
    pallas_call x1, Pallas kernels, body(): pl.pallas_call(functools.partial(kernel, n_row, n_col, factor), out_shape...  32.9 us
    pallas_call x1, Pallas kernels, body(): pl.pallas_call(write_out, out_shape=shapes, in_specs=[vmem] * 5, out_spec...  1.8 us

profile of v3, /device:TPU:0, one launch (start us, length us, event | category | flops | bytes accessed | tf_op | source)
XLA Modules:
  0.0 36.0 jit_solution(11723419166919179247)
XLA Ops:
  1.3 32.9 %shard_map.119 = (bf16[128,256]{1,0:T(8,128)(2,1)}, bf16[128,128]{1,0:T(8,128)(2,1)}, f32[128,256]{1,0:T(8,128)}, f32[128,256]{1,0:T(8,128)}, f32[256]{0:T(256)}) custom-call(bf16[128,128]{1,0:T(8,128)(2,1)} %feat.1, bf16[1,1,12,128,128]{4,3,2,1,0:T(8,128)(2,1)} %adj.1, s32[1,1,12]{2,1,0:T(1,128)} %pos_h.1, s32[1,1,1]{2,1,0:T(1,128)} %bitcast.1.cnt_h, ...), custom_call_target="tpu_custom_call" | custom-call | tf_op jit(solution)/shard_map/pallas_call | solution.py:346
  34.2 1.8 %shard_map.120 = (bf16[128,256]{1,0:T(8,128)(2,1)}, bf16[128,128]{1,0:T(8,128)(2,1)}, f32[128,256]{1,0:T(8,128)}, f32[128,256]{1,0:T(8,128)}, f32[256]{0:T(256)}) custom-call(bf16[128,256]{1,0:T(8,128)(2,1)} %get-tuple-element.10.refs_0_, bf16[128,128]{1,0:T(8,128)(2,1)} %get-tuple-element.11.refs_1_, f32[128,256]{1,0:T(8,128)} %get-tuple-element.12.refs_2_, ...), custom_call_target="tpu_custom_call" | custom-call | tf_op jit(solution)/shard_map/pallas_call | solution.py:356
